TPU v7x, 512 devices: a whole 4x4x16 slice. The times are simulated.
512 devices in a mesh: seq: 32 (over x, z_lo), fsdp: 16 (over y, z_hi, core).
Axes of the slice: x: 4, y: 4, z: 16 (z_hi: 2, z_lo: 8; z = z_hi * 8 + z_lo), core: 2. Of those that a mesh axis runs over, the one named last changes fastest.
Arguments:
- qkv: bfloat16 [16, 8192, 6144], P('fsdp', 'seq'), may hold values from -6 to 6
- resid: bfloat16 [16, 8192, 2048], P('fsdp', 'seq'), may hold values from -40 to 40
- targets: int32 [16, 8192], P('fsdp', 'seq'), may hold values from 0 to 511
- short_filter: float32 [7, 6144], replicated, may hold values from -2 to 2
- long_filter: bfloat16 [128, 128], replicated, may hold values from -0.5 to 0.5
- skip: float32 [2048], replicated, may hold values from -3 to 3
- out_weight: bfloat16 [2048, 2048], P('fsdp'), may hold values from -0.125 to 0.125
- gain: float32 [2048], replicated, may hold values from 0.1 to 1.9
- vocab_weight: bfloat16 [512, 2048], P('fsdp'), may hold values from -64 to 64
Outputs:
- logprob: float32 [16, 8192], P('fsdp', 'seq')
All inputs are finite; a program needn't handle non-finite values.
Results may differ from a plain program's by a relative error of at most 0.0022.
Values may be sent and summed in bfloat16 or wider, within the bound.
A program may use at most 128 MiB of HBM per device.

v0:
```python
import jax
import jax.numpy as jnp
from jax import lax
from jax.sharding import PartitionSpec as P


def shifted(shard, axis, by):
    length = lax.axis_size(axis)
    pairs = [(i, i + by) for i in range(length) if 0 <= i + by < length]
    return lax.ppermute(shard, axis, pairs)


def short_conv(extended, taps):
    count = extended.shape[0] - 6
    total = jnp.zeros((count, extended.shape[1]), jnp.float32)
    for lag in range(7):
        total = total + taps[lag] * extended[6 - lag : 6 - lag + count].astype(jnp.float32)
    return total


def toeplitz(taps):
    groups = taps.shape[0]
    flipped = taps[:, ::-1]
    padded = jnp.concatenate(
        [jnp.zeros((groups, 1), taps.dtype), flipped, jnp.zeros((groups, 128), taps.dtype)], axis=1
    )
    tiled = jnp.tile(padded, (1, 128))[:, : 128 * 256]
    return tiled.reshape(groups, 128, 256)


def long_conv(extended, matrix):
    blocks = extended.shape[0] // 128 - 1
    channels = extended.shape[1]
    groups = matrix.shape[0]
    pieces = extended.reshape(blocks + 1, 128, groups, channels // groups)
    pairs = jnp.concatenate([pieces[:-1], pieces[1:]], axis=1)
    result = jnp.einsum("gij,bjgc->bigc", matrix, pairs, preferred_element_type=jnp.float32)
    return result.reshape(blocks * 128, channels)


def body(qkv, resid, targets, short_filter, long_filter, skip, out_weight, gain, vocab_weight):
    rows = qkv[0]
    slab = rows.shape[0]
    hidden = skip.shape[0]
    matrix = toeplitz(long_filter)
    blank = jnp.zeros((1, hidden), jnp.bfloat16)
    kv_tail = rows[slab - 133 :, hidden:]
    q_tail = rows[slab - 6 :, :hidden]
    kv_prev, q_prev = shifted((kv_tail, q_tail), "seq", 1)
    kv_feat = short_conv(
        jnp.concatenate([kv_prev, rows[:, hidden:]], axis=0), short_filter[:, hidden:]
    )
    query = short_conv(
        jnp.concatenate([q_prev, rows[:, :hidden]], axis=0), short_filter[:, :hidden]
    )
    product = (kv_feat[:, :hidden] * kv_feat[:, hidden:]).astype(jnp.bfloat16)
    local = product[127:]
    longer = jnp.concatenate([blank, product], axis=0)
    wave = long_conv(longer, matrix) + skip * local.astype(jnp.float32)
    gated = (query * wave).astype(jnp.bfloat16)
    projected = jnp.dot(
        gated,
        lax.all_gather(out_weight, "fsdp", axis=0, tiled=True),
        preferred_element_type=jnp.float32,
    )
    stream = resid[0].astype(jnp.float32) + projected
    scale = lax.rsqrt(jnp.mean(stream * stream, axis=-1, keepdims=True) + 1e-05)
    normed = (stream * scale * gain).astype(jnp.bfloat16)
    logits = lax.dot_general(
        normed,
        lax.all_gather(vocab_weight, "fsdp", axis=0, tiled=True),
        (((1,), (1,)), ((), ())),
        preferred_element_type=jnp.float32,
    )
    top = jnp.max(logits, axis=-1, keepdims=True)
    total = top[:, 0] + jnp.log(jnp.sum(jnp.exp(logits - top), axis=-1))
    column = lax.broadcasted_iota(jnp.int32, logits.shape, 1)
    picked = jnp.sum(jnp.where(column == targets[0][:, None], logits, 0.0), axis=-1)
    return (picked - total)[None]


def solution(mesh):
    in_specs = (
        P("fsdp", "seq", None),
        P("fsdp", "seq", None),
        P("fsdp", "seq"),
        P(),
        P(),
        P(),
        P("fsdp", None),
        P(),
        P("fsdp", None),
    )
    out_specs = P("fsdp", "seq")
    return jax.shard_map(body, mesh=mesh, in_specs=in_specs, out_specs=out_specs, check_vma=False)
```

profile of v0, /device:TPU:1, one launch (start us, length us, event | category | flops | bytes accessed | tf_op | source)
XLA Modules:
  0.0 323.5 jit_solution(10514464192563160987)
XLA Ops:
  6.5 0.7 all-gather.3.cloned.1.call-update
  7.3 3.2 copy.16
  10.5 2.4 slice.182
  12.8 3.7 %copy.17 = bf16[133,4096]{1,0:T(8,128)(2,1)} copy(bf16[133,4096]{0,1:T(8,128)(2,1)} %slice.182) | data formatting | bytes 2179072 | tf_op jit(solution)/shard_map/slice | solution.py:47
  16.5 5.4 %collective-permute-start.1 = (bf16[133,4096]{1,0:T(8,128)(2,1)}, bf16[133,4096]{1,0:T(8,128)(2,1)}, u32[]{:S(2)}, u32[]{:S(2)}) collective-permute-start(bf16[133,4096]{1,0:T(8,128)(2,1)} %copy.17), channel_id=1, source_target_pairs={{0,16},{16,32},{32,48},{48,64},{64,80},{80,96},{96,112},{112,128},... | collective-permute-start | bytes 3268616 | tf_op jit(solution)/shard_map/ppermute | solution.py:10
  21.9 1.0 slice.171
  22.9 3.3 %collective-permute-start = (bf16[6,2048]{0,1:T(8,128)(2,1)}, bf16[6,2048]{0,1:T(8,128)(2,1)}, u32[]{:S(2)}, u32[]{:S(2)}) collective-permute-start(bf16[6,2048]{0,1:T(8,128)(2,1)} %slice.171), channel_id=1, source_target_pairs={{0,16},{16,32},{32,48},{48,64},{64,80},{80,96},{96,112},{112,128},... | collective-permute-start | bytes 73736 | tf_op jit(solution)/shard_map/ppermute | solution.py:10
  26.3 1.5 slice.183
  27.8 1.0 slice.170
  28.9 0.1 rev.3
  29.1 0.1 maximum_maximum_fusion
  29.2 0.1 copy.21
  29.3 4.5 %tile.4 = bf16[128,128,257]{0,2,1:T(8,128)(2,1)} broadcast(bf16[128,257]{0,1:T(8,128)(2,1)S(1)} %copy.21), dimensions={0,2} | broadcast | bytes 8487168 | tf_op jit(solution)/shard_map/tile | solution.py:27
  33.8 13.0 %tile.10 = bf16[128,32896]{0,1:T(8,128)(2,1)} reshape(bf16[128,128,257]{0,2,1:T(8,128)(2,1)} %tile.4) | data formatting | bytes 16842752 | tf_op jit(solution)/shard_map/tile | solution.py:27
  46.7 7.1 %slice.199 = bf16[128,32768]{0,1:T(8,128)(2,1)} slice(bf16[128,32896]{0,1:T(8,128)(2,1)} %tile.10), slice={[0:128], [0:32768]} | slice | bytes 16777216 | tf_op jit(solution)/shard_map/slice | solution.py:27
  53.8 12.6 %copy.24 = bf16[128,128,256,1]{2,1,3,0:T(8,128)(2,1)} copy(bf16[128,128,256,1]{0,2,1,3:T(8,128)(2,1)} %bitcast.48) | data formatting | bytes 16777216 | tf_op jit(solution)/shard_map/reshape | solution.py:28
  66.5 3.8 %copy.18 = bf16[133,4096]{0,1:T(8,128)(2,1)} copy(bf16[133,4096]{1,0:T(8,128)(2,1)} %collective-permute-done.1) | data formatting | bytes 2179072 | tf_op jit(solution)/shard_map/ppermute | solution.py:10
  70.2 17.8 %multiply_add_fusion = f32[383,4096]{0,1:T(8,128)S(1)} fusion(bf16[133,4096]{0,1:T(8,128)(2,1)} %copy.18, bf16[256,4096]{0,1:T(8,128)(2,1)S(1)} %copy-done, f32[4096]{0:T(1024)S(1)} %bitcast.59, f32[4096]{0:T(1024)S(1)} %bitcast.60, f32[4096]{0:T(1024)S(1)} %bitcast.55, f32[4096]{0:T(1024)S(1)} %bitcast.56, f32[4096]{0:T(1024)S(1)} %bitcast.57, ...), kind=kLoop, calls=%fused_computation.12 | loop fusion | flops 64319488 | bytes 9576448 | tf_op jit(solution)/shard_map/add | solution.py:17
  88.1 0.3 fusion.6
  88.4 1.8 pad_slice_fusion.22
  90.2 1.1 slice.166
  91.4 1.4 copy.19
  92.8 2.2 slice.168
  94.9 1.4 copy.20
  96.3 6.3 %fusion.13 = f32[2,128,128,16]{1,3,0,2:T(8,128)S(1)} fusion(bf16[128,128,256,1]{2,1,3,0:T(8,128)(2,1)} %copy.24, bf16[2,128,128,16]{1,3,0,2:T(8,128)(2,1)S(1)} %copy.20, bf16[2,128,128,16]{1,3,0,2:T(8,128)(2,1)S(1)} %copy.19), kind=kOutput, calls=%fused_computation.42 | convolution fusion | flops 272629760 | bytes 12582912 | tf_op jit(solution)/shard_map/gij,bjgc->bigc/dot_general | solution.py:37
  102.7 2.5 copy.23
  105.2 121.6 %all-gather.3.cloned.1.call-done = bf16[2048,2048]{1,0:T(8,128)(2,1)} async-done(((bf16[128,2048]{1,0:T(8,128)(2,1)}), bf16[2048,2048]{1,0:T(8,128)(2,1)}) %all-gather.3.cloned.1.call-update) | async-done | bytes 8388624 | tf_op jit(solution)/shard_map/all_gather | solution.py:63
  226.8 12.4 %multiply_reduce_fusion = (f32[256]{0:T(256)S(1)}, f32[256,2048]{1,0:T(8,128)}) fusion(bf16[2048,2048]{1,0:T(8,128)(2,1)} %all-gather.3.cloned.1.call-done, f32[256,8,2,128]{3,2,1,0:T(2,128)} %bitcast.53, bf16[256,2048]{0,1:T(8,128)(2,1)S(1)} %copy-done.1, bf16[6,2048]{0,1:T(8,128)(2,1)} %collective-permute-done, f32[2048]{0:T(1024)S(1)} %copy-done.6, ...), kind=kOutput, calls=%fused_computation.36 | convolution fusion | flops 2172124928 | bytes 15819776 | tf_op jit(solution)/shard_map/dot_general | solution.py:61
  239.2 73.5 %all-gather.5.cloned.1.call-done = bf16[512,2048]{1,0:T(8,128)(2,1)} async-done(((bf16[32,2048]{1,0:T(8,128)(2,1)}), bf16[512,2048]{1,0:T(8,128)(2,1)}) %all-gather.5.cloned.1.call-update) | async-done | bytes 2097168 | tf_op jit(solution)/shard_map/all_gather | solution.py:71
  312.7 3.1 fusion.39
  315.7 0.3 exponential_reduce_fusion
  316.0 0.6 add_subtract_fusion
  (25 shorter events, 0.3 us)
Async XLA Ops:
  6.5 220.3 %all-gather.3.cloned.1.call-start = ((), (), s32[]{:S(2)}) async-start(), calls=%async_computation | async-start | bytes 8912896 | tf_op jit(solution)/shard_map/all_gather | solution.py:63
  7.3 305.4 %all-gather.5.cloned.1.call-start = ((), (), s32[]{:S(2)}) async-start(), calls=%async_computation.1 | async-start | bytes 2228224 | tf_op jit(solution)/shard_map/all_gather | solution.py:71
  16.5 49.9 %collective-permute-start.1 = (bf16[133,4096]{1,0:T(8,128)(2,1)}, bf16[133,4096]{1,0:T(8,128)(2,1)}, u32[]{:S(2)}, u32[]{:S(2)}) collective-permute-start(bf16[133,4096]{1,0:T(8,128)(2,1)} %copy.17), channel_id=1, source_target_pairs={{0,16},{16,32},{32,48},{48,64},{64,80},{80,96},{96,112},{112,128},... | collective-permute-start | bytes 3268616 | tf_op jit(solution)/shard_map/ppermute | solution.py:10
  22.9 82.2 %collective-permute-start = (bf16[6,2048]{0,1:T(8,128)(2,1)}, bf16[6,2048]{0,1:T(8,128)(2,1)}, u32[]{:S(2)}, u32[]{:S(2)}) collective-permute-start(bf16[6,2048]{0,1:T(8,128)(2,1)} %slice.171), channel_id=1, source_target_pairs={{0,16},{16,32},{32,48},{48,64},{64,80},{80,96},{96,112},{112,128},... | collective-permute-start | bytes 73736 | tf_op jit(solution)/shard_map/ppermute | solution.py:10
  27.8 1.0 copy-start.3
  27.8 1.2 copy-start.2
  66.4 3.9 %copy-start = (bf16[256,4096]{0,1:T(8,128)(2,1)S(1)}, bf16[256,4096]{0,1:T(8,128)(2,1)}, u32[]{:S(2)}) copy-start(bf16[256,4096]{0,1:T(8,128)(2,1)} %slice.183) | copy-start | bytes 6291460
  102.7 124.1 %copy-start.1 = (bf16[256,2048]{0,1:T(8,128)(2,1)S(1)}, bf16[256,2048]{0,1:T(8,128)(2,1)}, u32[]{:S(2)}) copy-start(bf16[256,2048]{0,1:T(8,128)(2,1)} %slice.170) | copy-start | bytes 3145732
  102.7 124.1 %copy-start.6 = (f32[2048]{0:T(1024)S(1)}, f32[2048]{0:T(1024)}, u32[]{:S(2)}) copy-start(f32[2048]{0:T(1024)} %param.14) | copy-start | bytes 24580
  226.8 85.8 %copy-start.4 = (f32[2048]{0:T(1024)S(1)}, f32[2048]{0:T(1024)}, u32[]{:S(2)}) copy-start(f32[2048]{0:T(1024)} %param.16) | copy-start | bytes 24580
  312.7 3.1 copy-start.5
Sparse Core Ops, SparseCore 0:
  10.6 216.1 all-gather.2
  230.1 82.5 all-gather.4
where the time goes:
time: 325 us; the launch traced here: 323 us
  waiting for transfers between devices  196 us (60%)
  local copies, waits for them, and re-layouts  64.5 us (20%)
  matrix products  21.8 us (7%)
  other arithmetic  19.1 us (6%)
  between operations  13.5 us (4%)
  starting transfers between devices  8.75 us (3%)
    all_gather x1, waiting for transfers between devices, body(): lax.all_gather(out_weight, 'fsdp', axis=0, tiled=True)  122 us
    all_gather x1, waiting for transfers between devices, body(): lax.all_gather(vocab_weight, 'fsdp', axis=0, tiled=True)  73.5 us
    add x1, other arithmetic, short_conv(): total + taps[lag] * extended[6 - lag:6 - lag + count].astype(jnp.float32)  17.8 us
    another operation x2, local copies, waits for them, and re-layouts, toeplitz(): tiled = jnp.tile(padded, (1, 128))[:, :128 * 256]  17.4 us
    reshape x1, local copies, waits for them, and re-layouts, toeplitz(): return tiled.reshape(groups, 128, 256)  12.6 us
    dot_general x1, matrix products, body(): jnp.dot(gated, lax.all_gather(out_weight, 'fsdp', axis=0, tiled=True), pr...  12.4 us
    ppermute x2, starting transfers between devices, shifted(): return lax.ppermute(shard, axis, pairs)  8.71 us
    slice x5, local copies, waits for them, and re-layouts, long_conv(): pairs = jnp.concatenate([pieces[:-1], pieces[1:]], axis=1)  7.94 us
  transfers between devices with their start and end apart: 4, of which 2 were waited for; matrix products, arithmetic and copies ran while one was open for 31% of the time, Pallas kernels for 0%

commit v1 on v0

v1 whole, which is shorter than its diff:
```python
import jax
import jax.numpy as jnp
from jax import lax
from jax.experimental import pallas as pl
from jax.experimental.pallas import tpu as pltpu
from jax.sharding import PartitionSpec as P

MESH = pl.DeviceIdType.MESH
BF = jnp.bfloat16
F32 = jnp.float32


def place(x, y, z, c):
    x, y, z = lax.rem(x + 4, 4), lax.rem(y + 4, 4), lax.rem(z + 16, 16)
    return (x * 8 + lax.rem(z, 8), (y * 2 + z // 8) * 2 + c)


def cols(start, size):
    return pl.ds(pl.multiple_of(start, 128), size)


def kernel(
    qkv, resid, targets, taps, longs, skip, ow, gain, vw, out,
    raw, ext, prod, query, flips, mats, gated, wbuf, vbuf, stream, base, local_sem, send_sem, recv_sem,
):
    s, f = lax.axis_index("seq"), lax.axis_index("fsdp")
    x, zl = s // 8, lax.rem(s, 8)
    y, h, c = f // 4, lax.rem(f // 2, 2), lax.rem(f, 2)
    o = 1 - h
    z = h * 8 + zl
    lo, hi = zl == 0, zl == 7
    xl, xs, yl, ys = 1 - c, c, c, 1 - c

    def longer(d):
        return place(x + d * xl, y + d * yl, z, c)

    def shorter(d):
        return place(x + d * xs, y + d * ys, z, c)

    sibling = (s, f + 1 - 2 * c)
    after, before = (lax.rem(s + 1, 32), f), (lax.rem(s + 31, 32), f)
    source = place(x, y, jnp.where(zl < 4, h * 8 - 1, h * 8 + 8), c)

    def across(d):
        return place(x, y, jnp.where(lo, z - d, z + d), c)

    edge = jnp.logical_or(lo, hi)

    barrier = pltpu.get_barrier_semaphore()

    def greet(device):
        pl.semaphore_signal(barrier, inc=1, device_id=device, device_id_type=MESH)

    for d in (1, 2, 3):
        greet(longer(d))
        greet(shorter(d))
    for device in (sibling, after, before, source):
        greet(device)

    @pl.when(edge)
    def _():
        for d in (1, 2, 3, 4):
            greet(across(d))

    def load(src, dst, k):
        copy = pltpu.make_async_copy(src, dst, local_sem.at[k])
        copy.start()
        return copy

    H = 2048
    load_k = load(qkv.at[0, :, H : 2 * H], raw.at[16:272, H : 2 * H], 0)
    load_v = load(qkv.at[0, :, 2 * H :], raw.at[16:272, 2 * H :], 1)
    load_q = load(qkv.at[0, :, :H], raw.at[16:272, :H], 2)
    load_w = load(ow, wbuf.at[y, h, c], 3)
    load_u = load(vw, vbuf.at[y, h, c], 4)
    load_r = load(resid.at[0], base, 5)

    count = [0]
    sent = []

    def send(pairs, device, slot=None):
        copies = []
        for k, (src, dst) in enumerate(pairs):
            n = count[0]
            count[0] += 1
            copies.append(
                pltpu.make_async_remote_copy(
                    src_ref=src, dst_ref=dst, send_sem=send_sem.at[n],
                    recv_sem=recv_sem.at[n if slot is None else slot + k],
                    device_id=device, device_id_type=MESH,
                )
            )
        return copies

    def start(copies):
        for copy in copies:
            copy.start()

    def arrive(copies):
        for copy in copies:
            copy.wait_recv()

    def leave(copies):
        for copy in copies:
            copy.wait_send()

    quarter = cols(x * 512, 512)
    mine = [(ow, wbuf.at[y, h, c]), (vw, vbuf.at[y, h, c])]

    def block(yy, hh):
        return [(b.at[yy, hh, c], b.at[yy, hh, c]) for b in (wbuf, vbuf)]

    def part(yy, hh, xx):
        k = cols(xx * 512, 512)
        return [(b.at[yy, hh, c, :, k], b.at[yy, hh, c, :, k]) for b in (wbuf, vbuf)]

    def column(hh, xx):
        k = cols(xx * 512, 512)
        return [(b.at[:, hh, c, :, k], b.at[:, hh, c, :, k]) for b in (wbuf, vbuf)]

    def back(a, d):
        return lax.rem(a + 4 - d, 4)

    quarter_mine = [(ow.at[:, quarter], wbuf.at[y, h, c, :, quarter]), (vw.at[:, quarter], vbuf.at[y, h, c, :, quarter])]

    edge_slot = count[0]
    cross = [send(quarter_mine, across(d), edge_slot) for d in (4, 3, 2, 1)]
    cross_in = send(part(y, o, x), source, edge_slot)
    heads = send([(qkv.at[0, 240:256], raw.at[0:16])], after)
    full = {d: send(mine, longer(d)) for d in (1, 3, 2)}
    first = {d: send(quarter_mine, shorter(d)) for d in (1, 3, 2)}
    second = {(k, d): send(part(back(y, k), h, x), longer(d)) for k in (1, 3, 2) for d in (1, 3, 2)}
    tails = send([(prod.at[256:384], prod.at[0:128])], after)
    spread = {d: send(part(y, o, x), shorter(d)) for d in (1, 3, 2)}
    wide0 = {d: send(column(o, x), longer(d)) for d in (1, 3, 2)}
    wide1 = {d: send(block(y, o), longer(d)) for d in (1, 3, 2)}
    mate = send(mine, sibling)
    mate_own = {d: send(block(back(y, d), h), sibling) for d in (1, 3, 2)}
    mate_cross0 = {d: send(column(o, back(x, d)), sibling) for d in (0, 1, 3, 2)}
    slots = count[0]
    mate_cross1 = {}
    for d in (0, 1, 3, 2):
        n = count[0]
        mate_cross1[d] = send(block(back(y, d), o), sibling)

    pl.semaphore_wait(barrier, 10 + jnp.where(edge, 4, 0))

    @pl.when(edge)
    def _():
        for copies in cross:
            start(copies)

    start(heads)

    @pl.when(c == 0)
    def _():
        for d in (1, 3, 2):
            start(first[d])

    @pl.when(c == 1)
    def _():
        for d in (1, 3, 2):
            start(full[d])

    start(mate)

    def conv(col, lane, top, spot):
        ext[spot] = raw[top : top + 144, cols(col, 128)].astype(F32)
        total = jnp.zeros((128, 128), F32)
        for lag in range(7):
            total = total + taps[lag : lag + 1, cols(col, 128)] * ext[spot, 16 - lag : 144 - lag]
        return total

    def product(j, top):
        lane = j * 128
        k = conv(H + lane, lane, top, 0)
        v = conv(2 * H + lane, lane, top, 1)
        prod[128 + top : 256 + top, cols(lane, 128)] = (k * v).astype(BF)

    load_k.wait()
    load_v.wait()

    @pl.loop(0, 16)
    def _(j):
        product(j, 128)

    start(tails)
    load_q.wait()
    arrive(heads)

    @pl.when(s == 0)
    def _():
        raw[0:16] = jnp.zeros((16, 3 * H), BF)

    @pl.when(c == 0)
    def _():
        for d in (1, 3, 2):
            arrive(first[d])
            for e in (1, 3, 2):
                start(second[d, e])

    @pl.loop(0, 16)
    def _(j):
        product(j, 0)
        lane = j * 128
        query[0:128, cols(lane, 128)] = conv(lane, lane, 0, 2)
        query[128:256, cols(lane, 128)] = conv(lane, lane, 128, 3)

    rows = lax.broadcasted_iota(jnp.int32, (128, 128), 0)
    lanes = lax.broadcasted_iota(jnp.int32, (128, 128), 1)
    turn = jnp.where(lax.rem(rows + lanes, 128) == 0, 1.0, 0.0).astype(BF)
    flips[...] = jnp.dot(longs[...], turn, preferred_element_type=F32)

    @pl.loop(0, 128)
    def _(g):
        spin = pltpu.roll(jnp.broadcast_to(flips[pl.ds(g, 1), :], (128, 128)), 0, 1, stride=1, stride_axis=0)
        at = pl.ds(pl.multiple_of(g * 128, 128), 128)
        mats[at, 0:128] = jnp.where(lanes > rows, spin, 0.0).astype(BF)
        mats[at, 128:256] = jnp.where(lanes > rows, 0.0, spin).astype(BF)

    arrive(cross_in)
    for d in (1, 3, 2):
        start(spread[d])

    @pl.when(c == 0)
    def _():
        for d in (1, 3, 2):
            for k in (1, 3, 2):
                arrive(second[k, d])
        for d in (1, 3, 2):
            start(mate_own[d])
        for d in (1, 3, 2):
            arrive(spread[d])
        for d in (1, 3, 2):
            start(wide0[d])
        start(mate_cross0[0])

    @pl.when(c == 1)
    def _():
        for d in (1, 3, 2):
            arrive(full[d])
            start(mate_own[d])
        for d in (1, 3, 2):
            arrive(spread[d])
        for d in (1, 3, 2):
            start(wide1[d])
        start(mate_cross1[0])

    arrive(tails)

    @pl.when(s == 0)
    def _():
        prod[0:128] = jnp.zeros((128, H), BF)

    group = lax.broadcasted_iota(jnp.int32, (128, 128), 1) // 16

    @pl.loop(0, 16)
    def _(j):
        lane = cols(j * 128, 128)
        pair = jnp.concatenate([prod[0:256, lane], prod[128:384, lane]], axis=1)
        spans = jnp.dot(mats[pl.ds(pl.multiple_of(j * 1024, 1024), 1024), :], pair, preferred_element_type=F32)
        for b in (0, 1):
            wave = spans[0:128, b * 128 : b * 128 + 128]
            for g in range(1, 8):
                wave = jnp.where(group == g, spans[g * 128 : g * 128 + 128, b * 128 : b * 128 + 128], wave)
            at = slice(b * 128, b * 128 + 128)
            wave = wave + skip[:, lane] * prod[b * 128 + 128 : b * 128 + 256, lane].astype(F32)
            gated[at, lane] = (query[at, lane] * wave).astype(BF)

    load_w.wait()
    load_u.wait()
    load_r.wait()

    def project(hh, n):
        total = None
        for yy in range(4):
            left = gated[:, cols((yy * 2 + hh) * 256, 256)]
            right = wbuf[yy, hh, :, :, cols(n * 256, 256)].reshape(256, 256)
            term = jnp.dot(left, right, preferred_element_type=F32)
            total = term if total is None else total + term
        return total

    arrive(mate)
    for d in (1, 3, 2):
        arrive(mate_own[d])

    @pl.loop(0, 8)
    def _(n):
        at = cols(n * 256, 256)
        stream[:, at] = base[:, at].astype(F32) + project(h, n)

    @pl.when(c == 0)
    def _():
        for d in (1, 3, 2):
            arrive(wide0[d])
            start(mate_cross0[d])
        for d in (0, 1, 3, 2):
            arrive(mate_cross1[d])

    @pl.when(c == 1)
    def _():
        for d in (1, 3, 2):
            arrive(wide1[d])
            start(mate_cross1[d])
        for d in (0, 1, 3, 2):
            arrive(mate_cross0[d])

    def close(n, squares):
        at = cols(n * 256, 256)
        total = stream[:, at] + project(o, n)
        stream[:, at] = total
        return squares + total[:, :128] * total[:, :128] + total[:, 128:] * total[:, 128:]

    squares = lax.fori_loop(0, 8, close, jnp.zeros((256, 128), F32))
    scale = lax.rsqrt(jnp.sum(squares, axis=1, keepdims=True) / 2048.0 + 1e-05)

    @pl.loop(0, 8)
    def _(n):
        at = cols(n * 256, 256)
        gated[:, at] = (stream[:, at] * scale * gain[:, at]).astype(BF)

    logits = lax.dot_general(
        vbuf[...].reshape(512, H), gated[...], (((1,), (1,)), ((), ())), preferred_element_type=F32
    )
    top = jnp.max(logits, axis=0, keepdims=True)
    total = top + jnp.log(jnp.sum(jnp.exp(logits - top), axis=0, keepdims=True))
    entry = lax.broadcasted_iota(jnp.int32, (512, 256), 0)
    out[...] = jnp.sum(jnp.where(entry == targets[...], logits, 0.0), axis=0, keepdims=True) - total

    @pl.when(edge)
    def _():
        for copies in cross:
            leave(copies)

    leave(heads)
    leave(tails)
    leave(mate)
    for d in (1, 2, 3):
        leave(spread[d])
        leave(mate_own[d])

    @pl.when(c == 0)
    def _():
        for d in (1, 3, 2):
            leave(first[d])
            for e in (1, 3, 2):
                leave(second[d, e])
            leave(wide0[d])
        for d in (0, 1, 2, 3):
            leave(mate_cross0[d])

    @pl.when(c == 1)
    def _():
        for d in (1, 3, 2):
            leave(full[d])
            leave(wide1[d])
        for d in (0, 1, 2, 3):
            leave(mate_cross1[d])


def body(qkv, resid, targets, short_filter, long_filter, skip, out_weight, gain, vocab_weight):
    vmem = pl.BlockSpec(memory_space=pltpu.VMEM)
    hbm = pl.BlockSpec(memory_space=pl.ANY)
    return pl.pallas_call(
        kernel,
        name="hyena_block",
        out_shape=jax.ShapeDtypeStruct((1, 256), F32),
        in_specs=[hbm, hbm, vmem, vmem, vmem, vmem, hbm, vmem, hbm],
        out_specs=vmem,
        scratch_shapes=[
            pltpu.VMEM((272, 6144), BF),
            pltpu.VMEM((4, 144, 128), F32),
            pltpu.VMEM((384, 2048), BF),
            pltpu.VMEM((256, 2048), F32),
            pltpu.VMEM((128, 128), F32),
            pltpu.VMEM((16384, 256), BF),
            pltpu.VMEM((256, 2048), BF),
            pltpu.VMEM((4, 2, 2, 128, 2048), BF),
            pltpu.VMEM((4, 2, 2, 32, 2048), BF),
            pltpu.VMEM((256, 2048), F32),
            pltpu.VMEM((256, 2048), BF),
            pltpu.SemaphoreType.DMA((6,)),
            pltpu.SemaphoreType.DMA((96,)),
            pltpu.SemaphoreType.DMA((96,)),
        ],
        compiler_params=pltpu.CompilerParams(
            collective_id=0, has_side_effects=True, vmem_limit_bytes=52 << 20
        ),
        cost_estimate=pl.CostEstimate(flops=7_000_000_000, bytes_accessed=20_000_000, transcendentals=131072),
    )(
        qkv, resid, targets, short_filter, long_filter, skip.reshape(1, -1), out_weight,
        gain.reshape(1, -1), vocab_weight,
    )


def solution(mesh):
    in_specs = (
        P("fsdp", "seq", None),
        P("fsdp", "seq", None),
        P("fsdp", "seq"),
        P(),
        P(),
        P(),
        P("fsdp", None),
        P(),
        P("fsdp", None),
    )
    out_specs = P("fsdp", "seq")
    return jax.shard_map(body, mesh=mesh, in_specs=in_specs, out_specs=out_specs, check_vma=False)
```

time: 325 us -> 92.7 us (0.29)
  waiting for transfers between devices: 196 us -> 0 us
  Pallas kernels: 0 us -> 84.7 us
  local copies, waits for them, and re-layouts: 64.5 us -> 7.49 us
  matrix products: 21.8 us -> 0 us
  other arithmetic: 19.1 us -> 0 us
  between operations: 13.5 us -> 0.02 us
  starting transfers between devices: 8.75 us -> 0 us
    all_gather x2 -> x0, waiting for transfers between devices: 195 us -> none  [the longest x1 122 us: body(): lax.all_gather(out_weight, 'fsdp', axis=0, tiled=True)]
    pallas_call x0 -> x1, Pallas kernels: none -> 84.7 us  [body(): pl.pallas_call(kernel, name='hyena_block', out_shape=jax.ShapeDtypeStruct...]
    slice x13 -> x0, local copies, waits for them, and re-layouts: 24.8 us -> none  [the longest x5 7.94 us: long_conv(): pairs = jnp.concatenate([pieces[:-1], pieces[1:]], axis=1)]
    dot_general x3 -> x0, matrix products: 21.8 us -> none  [the longest x1 12.4 us: body(): jnp.dot(gated, lax.all_gather(out_weight, 'fsdp', axis=0, tiled=True), pr...]
    add x1 -> x0, other arithmetic: 17.8 us -> none  [short_conv(): total + taps[lag] * extended[6 - lag:6 - lag + count].astype(jnp.float32)]
    another operation x2 -> x0, local copies, waits for them, and re-layouts: 17.4 us -> none  [toeplitz(): tiled = jnp.tile(padded, (1, 128))[:, :128 * 256]]
    reshape x1 -> x0, local copies, waits for them, and re-layouts: 12.6 us -> none  [toeplitz(): return tiled.reshape(groups, 128, 256)]
    ppermute x2 -> x0, starting transfers between devices: 8.71 us -> none  [shifted(): return lax.ppermute(shard, axis, pairs)]
  transfers between devices with their start and end apart: 4 -> 0, of which waited for: 2 -> 0; matrix products, arithmetic and copies ran while one was open for 31% -> 0% of each run, Pallas kernels for 0% -> 0%
where the time goes in v1:
time: 92.7 us; the launch traced here: 92.2 us
  Pallas kernels  84.7 us (91%)
  local copies, waits for them, and re-layouts  7.49 us (8%)
    pallas_call x1, Pallas kernels, body(): pl.pallas_call(kernel, name='hyena_block', out_shape=jax.ShapeDtypeStruct...  84.7 us
    unnamed x17, local copies, waits for them, and re-layouts  7.49 us

profile of v1, /device:TPU:1, one launch (start us, length us, event | category | flops | bytes accessed | tf_op | source)
XLA Modules:
  0.0 92.2 jit_solution(3789526028972021184)
XLA Ops:
  0.0 0.0 copy-start
  0.0 1.2 %copy-done = bf16[1,256,2048]{2,1,0:T(8,128)(2,1)S(1)} copy-done((bf16[1,256,2048]{2,1,0:T(8,128)(2,1)S(1)}, bf16[1,256,2048]{2,1,0:T(8,128)(2,1)}, u32[]{:S(2)}) %copy-start) | copy-done | bytes 1048600
  1.2 0.0 copy-start.1
  1.2 1.0 %copy-done.1 = bf16[128,2048]{1,0:T(8,128)(2,1)S(1)} copy-done((bf16[128,2048]{1,0:T(8,128)(2,1)S(1)}, bf16[128,2048]{1,0:T(8,128)(2,1)}, u32[]{:S(2)}) %copy-start.1) | copy-done | bytes 524312
  2.3 0.0 copy-start.2
  2.3 0.9 %copy-done.2 = f32[7,6144]{1,0:T(8,128)S(1)} copy-done((f32[7,6144]{1,0:T(8,128)S(1)}, f32[7,6144]{1,0:T(8,128)}, u32[]{:S(2)}) %copy-start.2) | copy-done | bytes 172056
  3.2 0.0 copy-start.3
  3.2 0.9 copy-done.3
  4.1 0.0 copy-start.4
  4.1 0.8 copy-done.4
  4.9 0.0 copy-start.5
  4.9 0.7 copy-done.5
  5.6 0.0 copy-start.6
  5.6 0.7 copy-done.6
  6.3 0.0 copy-start.7
  6.3 0.7 copy-done.7
  6.9 84.7 %hyena_block.1 = f32[1,256]{1,0:T(1,128)S(1)} custom-call(bf16[1,256,6144]{2,1,0:T(8,128)(2,1)} %qkv.1, bf16[1,256,2048]{2,1,0:T(8,128)(2,1)S(1)} %copy-done, s32[1,256]{1,0:T(1,128)S(1)} %copy-done.7, f32[7,6144]{1,0:T(8,128)S(1)} %copy-done.2, bf16[128,128]{1,0:T(8,128)(2,1)S(1)} %copy-done.4, f32[1,2048]{1,0:T(1,128)S(1)} %bitcast.2, ...), custom_call_target="tpu_custom_call" | custom-call | flops 7000000000 | bytes 20000000 | tf_op jit(solution)/shard_map/hyena_block/pallas_call | solution.py:364
  91.6 0.6 copy.11
Async XLA Ops:
  0.0 1.2 %copy-start = (bf16[1,256,2048]{2,1,0:T(8,128)(2,1)S(1)}, bf16[1,256,2048]{2,1,0:T(8,128)(2,1)}, u32[]{:S(2)}) copy-start(bf16[1,256,2048]{2,1,0:T(8,128)(2,1)} %resid.1) | copy-start | bytes 3145732
  1.2 1.0 %copy-start.1 = (bf16[128,2048]{1,0:T(8,128)(2,1)S(1)}, bf16[128,2048]{1,0:T(8,128)(2,1)}, u32[]{:S(2)}) copy-start(bf16[128,2048]{1,0:T(8,128)(2,1)} %ow.1) | copy-start | bytes 1572868
  2.3 0.9 %copy-start.2 = (f32[7,6144]{1,0:T(8,128)S(1)}, f32[7,6144]{1,0:T(8,128)}, u32[]{:S(2)}) copy-start(f32[7,6144]{1,0:T(8,128)} %taps.1) | copy-start | bytes 516100
  3.2 0.9 copy-start.3
  4.1 0.8 copy-start.4
  4.9 0.7 copy-start.5
  5.6 0.7 copy-start.6
  6.3 0.7 copy-start.7

commit v2 on v0

v2 whole, which is shorter than its diff:
```python
import jax
import jax.numpy as jnp
from jax import lax
from jax.experimental import pallas as pl
from jax.experimental.pallas import tpu as pltpu
from jax.sharding import PartitionSpec as P

MESH = pl.DeviceIdType.MESH
BF = jnp.bfloat16
F32 = jnp.float32


def place(x, y, z, c):
    x, y, z = lax.rem(x + 4, 4), lax.rem(y + 4, 4), lax.rem(z + 16, 16)
    return (x * 8 + lax.rem(z, 8), (y * 2 + z // 8) * 2 + c)


def cols(start, size):
    return pl.ds(pl.multiple_of(start, 128), size)


def kernel(
    qkv, resid, targets, taps_in, longs_in, skip_in, ow, gain_in, vw, out,
    raw, ext, prod, query, flips, mats, gated, wbuf, stream, base, taps, longs, skip, gain, wanted,
    local_sem, send_sem, recv_sem,
):
    H = 2048
    s, f = lax.axis_index("seq"), lax.axis_index("fsdp")
    x, zl = s // 8, lax.rem(s, 8)
    y, h, c = f // 4, lax.rem(f // 2, 2), lax.rem(f, 2)
    o = 1 - h
    z = h * 8 + zl
    lo, hi = zl == 0, zl == 7
    edge = jnp.logical_or(lo, hi)
    rank = jnp.where(zl < 5, zl, 7 - zl)
    outward = jnp.where(zl < 5, -1, 1)
    passes = jnp.logical_or(zl < 4, zl > 5)

    def xpeer(d):
        return place(x + d, y, z, c)

    def ypeer(d):
        return place(x, y + d, z, c)

    def back(a, d):
        return lax.rem(a + 4 - d, 4)

    outer, inner = place(x, y, z + outward, c), place(x, y, z - outward, c)
    sibling = (s, f + 1 - 2 * c)
    after, before = (lax.rem(s + 1, 32), f), (lax.rem(s + 31, 32), f)
    around, near = (1, 3, 2), (1, 3)

    barrier = pltpu.get_barrier_semaphore()

    def greet(device):
        pl.semaphore_signal(barrier, inc=1, device_id=device, device_id_type=MESH)

    for d in around:
        greet(xpeer(d))
        greet(ypeer(d))
    for device in (sibling, after, before, outer):
        greet(device)

    @pl.when(passes)
    def _():
        greet(inner)

    loads = []

    def load(src, dst):
        copy = pltpu.make_async_copy(src, dst, local_sem.at[len(loads)])
        copy.start()
        loads.append(copy)
        return copy

    def own(half, strip):
        at = pl.ds(strip * 512 + half * 256, 256)
        return [
            load(ow.at[:, at], wbuf.at[y, h, c, half, strip, 0:128]),
            load(vw.at[:, at], wbuf.at[y, h, c, half, strip, 128:160]),
        ]

    load_own = [copy for half in (1, 0) for strip in range(4) for copy in own(half, strip)]
    load_late = load(qkv.at[0, 112:256, H:], raw.at[128:272, H:])
    load_taps = load(taps_in, taps)
    load_early = load(qkv.at[0, 0:112, H:], raw.at[16:128, H:])
    load_q = load(qkv.at[0, :, :H], raw.at[16:272, :H])
    load_rest = [
        load(longs_in, longs), load(skip_in, skip), load(gain_in, gain), load(targets, wanted), load(resid.at[0], base),
    ]

    count = [0]

    def send(src, device, dst=None, slot=None):
        n = count[0]
        count[0] += 1
        return pltpu.make_async_remote_copy(
            src_ref=src, dst_ref=src if dst is None else dst, send_sem=send_sem.at[n],
            recv_sem=recv_sem.at[n if slot is None else slot], device_id=device, device_id_type=MESH,
        )

    def strip(yy, hh, half, xx):
        return wbuf.at[yy, hh, c, half, xx]

    def whole(yy, hh, half):
        return wbuf.at[yy, hh, c, half]

    def column(hh, half, xx):
        return wbuf.at[:, hh, c, half, xx]

    def half_whole(yy, hh, d):
        return wbuf.at[yy, hh, c, 0, 0:2] if d == 1 else wbuf.at[yy, hh, c, 0, 2:4]

    def half_column(xx, d):
        return wbuf.at[0:2, o, c, 1, xx] if d == 1 else wbuf.at[2:4, o, c, 1, xx]

    def piece(hh, k):
        return wbuf.at[y, hh, c, k // 2, x, pl.ds(k % 2 * 80, 80)]

    cross, onward = [], []
    for k in range(4):
        slot = count[0]
        cross.append(send(piece(h, k), outer, slot=slot))
        onward.append(send(piece(o, k), inner, slot=slot))
    heads = send(qkv.at[0, 240:256], after, dst=raw.at[0:16])
    tails = [send(prod.at[256:384, k], after, dst=prod.at[0:128, k]) for k in (pl.ds(0, 1024), pl.ds(1024, 1024))]
    first = {d: send(strip(y, h, 1, x), ypeer(d)) for d in around}
    second = {(k, d): send(strip(back(y, k), h, 1, x), xpeer(d)) for k in around for d in around}
    direct = {d: send(whole(y, h, 0), ypeer(d)) for d in near}
    relay = {d: send(half_whole(back(y, d), h, d), ypeer(d)) for d in near}
    spread0 = {d: send(strip(y, o, 0, x), xpeer(d)) for d in around}
    spread1 = {d: send(strip(y, o, 1, x), ypeer(d)) for d in around}
    wide0 = {d: send(whole(y, o, 0), ypeer(d)) for d in near}
    wide1 = {d: send(column(o, 1, x), xpeer(d)) for d in near}
    relay0 = {d: send(half_whole(back(y, d), o, d), ypeer(d)) for d in near}
    relay1 = {d: send(half_column(back(x, d), d), xpeer(d)) for d in near}
    mate = send(wbuf.at[y, h, c], sibling)
    mate_direct = {d: send(whole(back(y, d), h, 0), sibling) for d in around}
    mate_second = {d: send(whole(back(y, d), h, 1), sibling) for d in around}
    mate_wide0 = {d: send(whole(back(y, d), o, 0), sibling) for d in (0,) + near}
    mate_wide1 = {d: send(column(o, 1, back(x, d)), sibling) for d in (0,) + near}
    mate_relay0 = {d: send(half_whole(back(y, 2), o, d), sibling) for d in near}
    mate_relay1 = {d: send(half_column(back(x, 2), d), sibling) for d in near}

    for copy in load_own:
        copy.wait()
    pl.semaphore_wait(barrier, 10 + jnp.where(passes, 1, 0))

    @pl.when(edge)
    def _():
        for copy in cross:
            copy.start()

    for d in around:
        first[d].start()
    def conv(col, top, spot):
        ext[spot] = raw[top : top + 144, cols(col, 128)].astype(F32)
        total = jnp.zeros((128, 128), F32)
        for lag in range(7):
            total = total + taps[lag : lag + 1, cols(col, 128)] * ext[spot, 16 - lag : 144 - lag]
        return total

    def product(lane, top, spot):
        k = conv(H + lane, top, spot)
        v = conv(2 * H + lane, top, spot + 1)
        prod[128 + top : 256 + top, cols(lane, 128)] = (k * v).astype(BF)

    load_late.wait()
    load_taps.wait()

    @pl.loop(0, 16)
    def _(j):
        product(j * 128, 128, 0)

    def hand_on(*copies):
        for copy in copies:
            copy.start()

    @pl.when(jnp.logical_or(zl == 3, jnp.logical_or(hi, jnp.logical_not(passes))))
    def _():
        hand_on(heads, tails[0])

    @pl.when(jnp.logical_or(hi, jnp.logical_not(passes)))
    def _():
        hand_on(tails[1])

    for d in near:
        direct[d].start()
    mate.start()

    def cross_over(level):
        @pl.when(rank == level)
        def _():
            for k in range(4):
                onward[k].wait_recv()
                if level < 4:
                    pl.when(passes)(onward[k].start)
                if k % 2:
                    for d in around:
                        (spread0, spread1)[k // 2][d].start()

    cross_over(0)

    @pl.when(lo)
    def _():
        hand_on(heads, *tails)

    for k in around:
        first[k].wait_recv()
        for d in around:
            second[k, d].start()

    cross_over(1)

    @pl.when(rank == 1)
    def _():
        hand_on(heads, *tails)

    rows = lax.broadcasted_iota(jnp.int32, (128, 128), 0)
    lanes = lax.broadcasted_iota(jnp.int32, (128, 128), 1)
    turn = jnp.where(lax.rem(rows + lanes, 128) == 0, 1.0, 0.0).astype(BF)
    load_rest[0].wait()
    flips[...] = jnp.dot(longs[...], turn, preferred_element_type=F32)

    @pl.loop(0, 16)
    def _(j):
        for k in range(8):
            g = j * 8 + k
            spin = pltpu.roll(jnp.broadcast_to(flips[pl.ds(g, 1), :], (128, 128)), 0, 1, stride=1, stride_axis=0)
            at = pl.ds(pl.multiple_of(g * 128, 128), 128)
            mats[at, 0:128] = jnp.where(lanes > rows, spin, 0.0).astype(BF)
            mats[at, 128:256] = jnp.where(lanes > rows, 0.0, spin).astype(BF)

    cross_over(2)

    @pl.when(zl == 2)
    def _():
        hand_on(heads, *tails)

    cross_over(3)

    @pl.when(zl == 3)
    def _():
        hand_on(tails[1])

    for d in near:
        direct[d].wait_recv()
        relay[d].start()
    cross_over(4)
    for d in near:
        mate_direct[d].start()
    for k in around:
        for d in around:
            second[k, d].wait_recv()
        mate_second[k].start()
    for d in around:
        spread0[d].wait_recv()
    for d in near:
        wide0[d].start()
    for d in around:
        spread1[d].wait_recv()
    for d in near:
        wide1[d].start()
    mate_wide0[0].start()
    mate_wide1[0].start()
    for d in near:
        relay[d].wait_recv()
    mate_direct[2].start()

    def pass_wide():
        for d in near:
            wide0[d].wait_recv()
            relay0[d].start()
            wide1[d].wait_recv()
            relay1[d].start()
        for d in near:
            mate_wide0[d].start()
            mate_wide1[d].start()

    hurry = jnp.logical_or(zl == 0, zl == 4)
    pl.when(hurry)(pass_wide)
    load_early.wait()
    load_q.wait()
    for copy in load_rest[1:]:
        copy.wait()
    heads.wait_recv()

    @pl.when(s == 0)
    def _():
        raw[0:16] = jnp.zeros((16, 3 * H), BF)

    @pl.loop(0, 16)
    def _(j):
        lane = j * 128
        product(lane, 0, 0)
        query[0:128, cols(lane, 128)] = conv(lane, 0, 2)
        query[128:256, cols(lane, 128)] = conv(lane, 128, 3)

    for copy in tails:
        copy.wait_recv()

    @pl.when(s == 0)
    def _():
        prod[0:128] = jnp.zeros((128, H), BF)

    group = lax.broadcasted_iota(jnp.int32, (128, 128), 1) // 16

    @pl.loop(0, 16)
    def _(j):
        lane = cols(j * 128, 128)
        pair = jnp.concatenate([prod[0:256, lane], prod[128:384, lane]], axis=1)
        spans = jnp.dot(mats[pl.ds(pl.multiple_of(j * 1024, 1024), 1024), :], pair, preferred_element_type=F32)
        for b in (0, 1):
            wave = spans[0:128, b * 128 : b * 128 + 128]
            for g in range(1, 8):
                wave = jnp.where(group == g, spans[g * 128 : g * 128 + 128, b * 128 : b * 128 + 128], wave)
            at = slice(b * 128, b * 128 + 128)
            wave = wave + skip[:, lane] * prod[b * 128 + 128 : b * 128 + 256, lane].astype(F32)
            gated[at, lane] = (query[at, lane] * wave).astype(BF)

    def project(hh, half, xx):
        left = jnp.concatenate([gated[:, cols((yy * 2 + hh) * 256, 256)] for yy in range(4)], axis=1)
        right = jnp.concatenate([wbuf[yy, hh, :, half, xx, 0:128, :].reshape(256, 256) for yy in range(4)], axis=0)
        return jnp.dot(left, right, preferred_element_type=F32)

    pl.when(jnp.logical_not(hurry))(pass_wide)
    mate.wait_recv()
    for d in around:
        mate_direct[d].wait_recv()
    for d in around:
        mate_second[d].wait_recv()

    @pl.loop(0, 8)
    def _(n):
        half, xx = n // 4, lax.rem(n, 4)
        at = cols(xx * 512 + half * 256, 256)
        stream[:, at] = base[:, at].astype(F32) + project(h, half, xx)

    for d in near:
        relay0[d].wait_recv()
        mate_relay0[d].start()
        relay1[d].wait_recv()
        mate_relay1[d].start()
    for group_of in (mate_wide0, mate_wide1, mate_relay0, mate_relay1):
        for copy in group_of.values():
            copy.wait_recv()

    def close(n, squares):
        half, xx = n // 4, lax.rem(n, 4)
        at = cols(xx * 512 + half * 256, 256)
        total = stream[:, at] + project(o, half, xx)
        stream[:, at] = total
        return squares + total[:, :128] * total[:, :128] + total[:, 128:] * total[:, 128:]

    squares = lax.fori_loop(0, 8, close, jnp.zeros((256, 128), F32))
    scale = lax.rsqrt(jnp.sum(squares, axis=1, keepdims=True) / 2048.0 + 1e-05)

    @pl.loop(0, 8)
    def _(n):
        at = cols(n * 256, 256)
        gated[:, at] = (stream[:, at] * scale * gain[:, at]).astype(BF)

    words = jnp.concatenate(
        [wbuf[:, :, :, n % 2, n // 2, 128:160, :].reshape(512, 256) for n in range(8)], axis=1
    )
    logits = lax.dot_general(words, gated[...], (((1,), (1,)), ((), ())), preferred_element_type=F32)
    top = jnp.max(logits, axis=0, keepdims=True)
    total = top + jnp.log(jnp.sum(jnp.exp(logits - top), axis=0, keepdims=True))
    entry = lax.broadcasted_iota(jnp.int32, (512, 256), 0)
    out[...] = jnp.sum(jnp.where(entry == wanted[...], logits, 0.0), axis=0, keepdims=True) - total

    @pl.when(edge)
    def _():
        for copy in cross:
            copy.wait_send()

    @pl.when(passes)
    def _():
        for copy in onward:
            copy.wait_send()

    for copy in (heads, *tails, mate):
        copy.wait_send()
    for group_of in (
        first, second, direct, relay, spread0, spread1, wide0, wide1, relay0, relay1, mate_direct, mate_second, mate_wide0, mate_wide1,
        mate_relay0, mate_relay1,
    ):
        for copy in group_of.values():
            copy.wait_send()


def body(qkv, resid, targets, short_filter, long_filter, skip, out_weight, gain, vocab_weight):
    vmem = pl.BlockSpec(memory_space=pltpu.VMEM)
    hbm = pl.BlockSpec(memory_space=pltpu.HBM)
    return pl.pallas_call(
        kernel,
        name="hyena_block",
        out_shape=jax.ShapeDtypeStruct((1, 256), F32),
        in_specs=[hbm] * 9,
        out_specs=vmem,
        scratch_shapes=[
            pltpu.VMEM((272, 6144), BF),
            pltpu.VMEM((4, 144, 128), F32),
            pltpu.VMEM((384, 2048), BF),
            pltpu.VMEM((256, 2048), F32),
            pltpu.VMEM((128, 128), F32),
            pltpu.VMEM((16384, 256), BF),
            pltpu.VMEM((256, 2048), BF),
            pltpu.VMEM((4, 2, 2, 2, 4, 160, 256), BF),
            pltpu.VMEM((256, 2048), F32),
            pltpu.VMEM((256, 2048), BF),
            pltpu.VMEM((7, 6144), F32),
            pltpu.VMEM((128, 128), BF),
            pltpu.VMEM((1, 2048), F32),
            pltpu.VMEM((1, 2048), F32),
            pltpu.VMEM((1, 256), jnp.int32),
            pltpu.SemaphoreType.DMA((32,)),
            pltpu.SemaphoreType.DMA((72,)),
            pltpu.SemaphoreType.DMA((72,)),
        ],
        compiler_params=pltpu.CompilerParams(
            collective_id=0, has_side_effects=True, vmem_limit_bytes=60 << 20
        ),
        cost_estimate=pl.CostEstimate(flops=7_000_000_000, bytes_accessed=20_000_000, transcendentals=131072),
    )(
        qkv, resid, targets, short_filter, long_filter, skip.reshape(1, -1), out_weight,
        gain.reshape(1, -1), vocab_weight,
    )


def solution(mesh):
    in_specs = (
        P("fsdp", "seq", None),
        P("fsdp", "seq", None),
        P("fsdp", "seq"),
        P(),
        P(),
        P(),
        P("fsdp", None),
        P(),
        P("fsdp", None),
    )
    out_specs = P("fsdp", "seq")
    return jax.shard_map(body, mesh=mesh, in_specs=in_specs, out_specs=out_specs, check_vma=False)
```

time: 325 us -> 81.1 us (0.25)
  waiting for transfers between devices: 196 us -> 0 us
  Pallas kernels: 0 us -> 79.7 us
  local copies, waits for them, and re-layouts: 64.5 us -> 1.24 us
  matrix products: 21.8 us -> 0 us
  other arithmetic: 19.1 us -> 0 us
  between operations: 13.5 us -> 0.01 us
  starting transfers between devices: 8.75 us -> 0 us
    all_gather x2 -> x0, waiting for transfers between devices: 195 us -> none  [the longest x1 122 us: body(): lax.all_gather(out_weight, 'fsdp', axis=0, tiled=True)]
    pallas_call x0 -> x1, Pallas kernels: none -> 79.7 us  [body(): pl.pallas_call(kernel, name='hyena_block', out_shape=jax.ShapeDtypeStruct...]
    slice x13 -> x0, local copies, waits for them, and re-layouts: 24.8 us -> none  [the longest x5 7.94 us: long_conv(): pairs = jnp.concatenate([pieces[:-1], pieces[1:]], axis=1)]
    dot_general x3 -> x0, matrix products: 21.8 us -> none  [the longest x1 12.4 us: body(): jnp.dot(gated, lax.all_gather(out_weight, 'fsdp', axis=0, tiled=True), pr...]
    add x1 -> x0, other arithmetic: 17.8 us -> none  [short_conv(): total + taps[lag] * extended[6 - lag:6 - lag + count].astype(jnp.float32)]
    another operation x2 -> x0, local copies, waits for them, and re-layouts: 17.4 us -> none  [toeplitz(): tiled = jnp.tile(padded, (1, 128))[:, :128 * 256]]
    reshape x1 -> x0, local copies, waits for them, and re-layouts: 12.6 us -> none  [toeplitz(): return tiled.reshape(groups, 128, 256)]
    ppermute x2 -> x0, starting transfers between devices: 8.71 us -> none  [shifted(): return lax.ppermute(shard, axis, pairs)]
  transfers between devices with their start and end apart: 4 -> 0, of which waited for: 2 -> 0; matrix products, arithmetic and copies ran while one was open for 31% -> 0% of each run, Pallas kernels for 0% -> 0%
where the time goes in v2:
time: 81.1 us; the launch traced here: 81 us
  Pallas kernels  79.7 us (98%)
  local copies, waits for them, and re-layouts  1.24 us (2%)
    pallas_call x1, Pallas kernels, body(): pl.pallas_call(kernel, name='hyena_block', out_shape=jax.ShapeDtypeStruct...  79.7 us

profile of v2, /device:TPU:1, one launch (start us, length us, event | category | flops | bytes accessed | tf_op | source)
XLA Modules:
  0.0 81.0 jit_solution(15254935379845026800)
XLA Ops:
  0.0 79.7 %hyena_block.1 = f32[1,256]{1,0:T(1,128)} custom-call(bf16[1,256,6144]{2,1,0:T(8,128)(2,1)} %qkv.1, bf16[1,256,2048]{2,1,0:T(8,128)(2,1)} %resid.1, s32[1,256]{1,0:T(1,128)} %targets.1, f32[7,6144]{1,0:T(8,128)} %taps_in.1, bf16[128,128]{1,0:T(8,128)(2,1)} %longs_in.1, f32[1,2048]{1,0:T(1,128)} %bitcast.2, bf16[128,2048]{1,0:T(8,128)(2,1)} %ow.1, ...), custom_call_target="tpu_custom_call" | custom-call | flops 7000000000 | bytes 20000000 | tf_op jit(solution)/shard_map/hyena_block/pallas_call | solution.py:395
  79.7 1.2 %copy.11 = f32[1,256]{1,0:T(1,128)} copy(f32[1,256]{1,0:T(1,128)} %hyena_block.1) | data formatting | bytes 2048

commit v3 on v2

--- a/solution.py
+++ b/solution.py
@@ -21,7 +21,7 @@
 
 def kernel(
     qkv, resid, targets, taps_in, longs_in, skip_in, ow, gain_in, vw, out,
-    raw, ext, prod, query, flips, mats, gated, wbuf, stream, base, taps, longs, skip, gain, wanted,
+    raw, ext, pack, prod, ferry, query, flips, mats, gated, wbuf, stream, base, taps, longs, skip, gain, wanted,
     local_sem, send_sem, recv_sem,
 ):
     H = 2048
@@ -65,6 +65,12 @@
     def _():
         greet(inner)
 
+    far = place(x, y, jnp.where(lo, z + 7, z - 7), c)
+
+    @pl.when(edge)
+    def _():
+        greet(far)
+
     loads = []
 
     def load(src, dst):
@@ -122,10 +128,17 @@
         slot = count[0]
         cross.append(send(piece(h, k), outer, slot=slot))
         onward.append(send(piece(o, k), inner, slot=slot))
-    heads = send(qkv.at[0, 240:256], after, dst=raw.at[0:16])
+    heads = send(pack.at[0], after, dst=pack.at[1])
     tails = [send(prod.at[256:384, k], after, dst=prod.at[0:128, k]) for k in (pl.ds(0, 1024), pl.ds(1024, 1024))]
+    ferry_out = send(prod.at[256:384, 1024:], xpeer(1), dst=ferry)
+    ferry_on = send(ferry, far, dst=prod.at[0:128, 1024:], slot=count[0] - 2)
     first = {d: send(strip(y, h, 1, x), ypeer(d)) for d in around}
-    second = {(k, d): send(strip(back(y, k), h, 1, x), xpeer(d)) for k in around for d in around}
+    second = {(k, d): send(strip(back(y, k), h, 1, x), xpeer(d)) for k in around for d in near}
+    second_on = {
+        (k, d): send(strip(back(y, k), h, 1, back(x, d)), xpeer(d)) for k, d in ((1, 1), (3, 3))
+    }
+    for d in near:
+        second_on[2, d] = send(wbuf.at[back(y, 2), h, c, 1, back(x, d), pl.ds(d // 2 * 80, 80)], xpeer(d))
     direct = {d: send(whole(y, h, 0), ypeer(d)) for d in near}
     relay = {d: send(half_whole(back(y, d), h, d), ypeer(d)) for d in near}
     spread0 = {d: send(strip(y, o, 0, x), xpeer(d)) for d in around}
@@ -144,7 +157,7 @@
 
     for copy in load_own:
         copy.wait()
-    pl.semaphore_wait(barrier, 10 + jnp.where(passes, 1, 0))
+    pl.semaphore_wait(barrier, 10 + jnp.where(passes, 1, 0) + jnp.where(edge, 1, 0))
 
     @pl.when(edge)
     def _():
@@ -167,6 +180,9 @@
 
     load_late.wait()
     load_taps.wait()
+    load_q.wait()
+    last = raw[256:272].astype(F32)[8:16]
+    pack[0] = jnp.concatenate([last[:, :3072], last[:, 3072:]], axis=0).astype(BF)
 
     @pl.loop(0, 16)
     def _(j):
@@ -176,11 +192,15 @@
         for copy in copies:
             copy.start()
 
-    @pl.when(jnp.logical_or(zl == 3, jnp.logical_or(hi, jnp.logical_not(passes))))
+    @pl.when(hi)
+    def _():
+        hand_on(ferry_out)
+
+    @pl.when(jnp.logical_or(zl == 3, jnp.logical_not(passes)))
     def _():
         hand_on(heads, tails[0])
 
-    @pl.when(jnp.logical_or(hi, jnp.logical_not(passes)))
+    @pl.when(jnp.logical_not(passes))
     def _():
         hand_on(tails[1])
 
@@ -207,7 +227,7 @@
 
     for k in around:
         first[k].wait_recv()
-        for d in around:
+        for d in near:
             second[k, d].start()
 
     cross_over(1)
@@ -243,24 +263,35 @@
     def _():
         hand_on(tails[1])
 
+    cross_over(4)
+    for copy in second.values():
+        copy.wait_recv()
+    for copy in second_on.values():
+        copy.start()
+
+    @pl.when(hi)
+    def _():
+        hand_on(heads, tails[0])
+        ferry_out.wait_recv()
+        ferry_on.start()
+
     for d in near:
         direct[d].wait_recv()
         relay[d].start()
-    cross_over(4)
     for d in near:
         mate_direct[d].start()
-    for k in around:
-        for d in around:
-            second[k, d].wait_recv()
-        mate_second[k].start()
+    for copy in second_on.values():
+        copy.wait_recv()
+    for d in around:
+        mate_second[d].start()
     for d in around:
         spread0[d].wait_recv()
     for d in near:
         wide0[d].start()
     for d in around:
         spread1[d].wait_recv()
-    for d in near:
-        wide1[d].start()
+    wide1[3].start()
+    pl.when(jnp.logical_not(lo))(wide1[1].start)
     mate_wide0[0].start()
     mate_wide1[0].start()
     for d in near:
@@ -277,17 +308,19 @@
             mate_wide0[d].start()
             mate_wide1[d].start()
 
-    hurry = jnp.logical_or(zl == 0, zl == 4)
-    pl.when(hurry)(pass_wide)
     load_early.wait()
-    load_q.wait()
     for copy in load_rest[1:]:
         copy.wait()
     heads.wait_recv()
-
-    @pl.when(s == 0)
-    def _():
-        raw[0:16] = jnp.zeros((16, 3 * H), BF)
+    got = jnp.where(s == 0, 0.0, pack[1].astype(F32))
+    raw[0:16, :3072] = jnp.concatenate([got[0:8], got[0:8]], axis=0).astype(BF)
+    raw[0:16, 3072:] = jnp.concatenate([got[8:16], got[8:16]], axis=0).astype(BF)
+
+    @pl.when(lo)
+    def _():
+        for copy in tails:
+            copy.wait_recv()
+        wide1[1].start()
 
     @pl.loop(0, 16)
     def _(j):
@@ -296,8 +329,10 @@
         query[0:128, cols(lane, 128)] = conv(lane, 0, 2)
         query[128:256, cols(lane, 128)] = conv(lane, 128, 3)
 
-    for copy in tails:
-        copy.wait_recv()
+    @pl.when(jnp.logical_not(lo))
+    def _():
+        for copy in tails:
+            copy.wait_recv()
 
     @pl.when(s == 0)
     def _():
@@ -318,12 +353,19 @@
             wave = wave + skip[:, lane] * prod[b * 128 + 128 : b * 128 + 256, lane].astype(F32)
             gated[at, lane] = (query[at, lane] * wave).astype(BF)
 
-    def project(hh, half, xx):
-        left = jnp.concatenate([gated[:, cols((yy * 2 + hh) * 256, 256)] for yy in range(4)], axis=1)
-        right = jnp.concatenate([wbuf[yy, hh, :, half, xx, 0:128, :].reshape(256, 256) for yy in range(4)], axis=0)
+    def tile(half, xx):
+        return cols(xx * 512 + half * 256, 256)
+
+    def project(hh, half, xx, blocks):
+        left = jnp.concatenate([gated[:, cols((yy * 2 + hh) * 256, 256)] for yy in blocks], axis=1)
+        right = jnp.concatenate([wbuf[yy, hh, :, half, xx, 0:128, :].reshape(256, 256) for yy in blocks], axis=0)
         return jnp.dot(left, right, preferred_element_type=F32)
 
-    pl.when(jnp.logical_not(hurry))(pass_wide)
+    def gather_in(half, xx, blocks):
+        at = tile(half, xx)
+        stream[:, at] = stream[:, at] + project(o, half, xx, blocks)
+
+    pass_wide()
     mate.wait_recv()
     for d in around:
         mate_direct[d].wait_recv()
@@ -333,26 +375,40 @@
     @pl.loop(0, 8)
     def _(n):
         half, xx = n // 4, lax.rem(n, 4)
-        at = cols(xx * 512 + half * 256, 256)
-        stream[:, at] = base[:, at].astype(F32) + project(h, half, xx)
+        at = tile(half, xx)
+        stream[:, at] = base[:, at].astype(F32) + project(h, half, xx, range(4))
+
+    for group_of in (mate_wide0, mate_wide1):
+        for copy in group_of.values():
+            copy.wait_recv()
+
+    @pl.loop(0, 3)
+    def _(n):
+        gather_in(1, lax.rem(x + 3 + n, 4), range(4))
+
+    @pl.loop(0, 4)
+    def _(n):
+        gather_in(0, n, [lax.rem(y + 3 + k, 4) for k in range(3)])
 
     for d in near:
         relay0[d].wait_recv()
         mate_relay0[d].start()
         relay1[d].wait_recv()
         mate_relay1[d].start()
-    for group_of in (mate_wide0, mate_wide1, mate_relay0, mate_relay1):
+    for group_of in (mate_relay0, mate_relay1):
         for copy in group_of.values():
             copy.wait_recv()
 
+    gather_in(1, lax.rem(x + 2, 4), range(4))
+
     def close(n, squares):
-        half, xx = n // 4, lax.rem(n, 4)
-        at = cols(xx * 512 + half * 256, 256)
-        total = stream[:, at] + project(o, half, xx)
-        stream[:, at] = total
-        return squares + total[:, :128] * total[:, :128] + total[:, 128:] * total[:, 128:]
-
-    squares = lax.fori_loop(0, 8, close, jnp.zeros((256, 128), F32))
+        gather_in(0, n, [lax.rem(y + 2, 4)])
+        for half in (0, 1):
+            total = stream[:, tile(half, n)]
+            squares = squares + total[:, :128] * total[:, :128] + total[:, 128:] * total[:, 128:]
+        return squares
+
+    squares = lax.fori_loop(0, 4, close, jnp.zeros((256, 128), F32))
     scale = lax.rsqrt(jnp.sum(squares, axis=1, keepdims=True) / 2048.0 + 1e-05)
 
     @pl.loop(0, 8)
@@ -379,10 +435,19 @@
         for copy in onward:
             copy.wait_send()
 
-    for copy in (heads, *tails, mate):
+    @pl.when(hi)
+    def _():
+        ferry_out.wait_send()
+        ferry_on.wait_send()
+
+    @pl.when(jnp.logical_not(hi))
+    def _():
+        tails[1].wait_send()
+
+    for copy in (heads, tails[0], mate):
         copy.wait_send()
     for group_of in (
-        first, second, direct, relay, spread0, spread1, wide0, wide1, relay0, relay1, mate_direct, mate_second, mate_wide0, mate_wide1,
+        first, second, second_on, direct, relay, spread0, spread1, wide0, wide1, relay0, relay1, mate_direct, mate_second, mate_wide0, mate_wide1,
         mate_relay0, mate_relay1,
     ):
         for copy in group_of.values():
@@ -401,7 +466,9 @@
         scratch_shapes=[
             pltpu.VMEM((272, 6144), BF),
             pltpu.VMEM((4, 144, 128), F32),
+            pltpu.VMEM((2, 16, 3072), BF),
             pltpu.VMEM((384, 2048), BF),
+            pltpu.VMEM((128, 1024), BF),
             pltpu.VMEM((256, 2048), F32),
             pltpu.VMEM((128, 128), F32),
             pltpu.VMEM((16384, 256), BF),

time: 81.1 us -> 70.8 us (0.87)
  Pallas kernels: 79.7 us -> 69.4 us
    pallas_call x1, Pallas kernels: 79.7 us -> 69.4 us  [body(): pl.pallas_call(kernel, name='hyena_block', out_shape=jax.ShapeDtypeStruct...]
where the time goes in v3:
time: 70.8 us; the launch traced here: 70.6 us
  Pallas kernels  69.4 us (98%)
  local copies, waits for them, and re-layouts  1.24 us (2%)
    pallas_call x1, Pallas kernels, body(): pl.pallas_call(kernel, name='hyena_block', out_shape=jax.ShapeDtypeStruct...  69.4 us

profile of v3, /device:TPU:1, one launch (start us, length us, event | category | flops | bytes accessed | tf_op | source)
XLA Modules:
  0.0 70.6 jit_solution(5447019970332293022)
XLA Ops:
  0.0 69.4 %hyena_block.1 = f32[1,256]{1,0:T(1,128)} custom-call(bf16[1,256,6144]{2,1,0:T(8,128)(2,1)} %qkv.1, bf16[1,256,2048]{2,1,0:T(8,128)(2,1)} %resid.1, s32[1,256]{1,0:T(1,128)} %targets.1, f32[7,6144]{1,0:T(8,128)} %taps_in.1, bf16[128,128]{1,0:T(8,128)(2,1)} %longs_in.1, f32[1,2048]{1,0:T(1,128)} %bitcast.2, bf16[128,2048]{1,0:T(8,128)(2,1)} %ow.1, ...), custom_call_target="tpu_custom_call" | custom-call | flops 7000000000 | bytes 20000000 | tf_op jit(solution)/shard_map/hyena_block/pallas_call | solution.py:460
  69.4 1.2 %copy.11 = f32[1,256]{1,0:T(1,128)} copy(f32[1,256]{1,0:T(1,128)} %hyena_block.1) | data formatting | bytes 2048

commit v4 on v3

--- a/solution.py
+++ b/solution.py
@@ -129,9 +129,12 @@
         cross.append(send(piece(h, k), outer, slot=slot))
         onward.append(send(piece(o, k), inner, slot=slot))
     heads = send(pack.at[0], after, dst=pack.at[1])
-    tails = [send(prod.at[256:384, k], after, dst=prod.at[0:128, k]) for k in (pl.ds(0, 1024), pl.ds(1024, 1024))]
-    ferry_out = send(prod.at[256:384, 1024:], xpeer(1), dst=ferry)
-    ferry_on = send(ferry, far, dst=prod.at[0:128, 1024:], slot=count[0] - 2)
+    tails, ferry_out, ferry_on = [], [], []
+    for k in (0, 1):
+        at, slot = pl.ds(k * 1024, 1024), count[0]
+        tails.append(send(prod.at[256:384, at], after, dst=prod.at[0:128, at]))
+        ferry_out.append(send(prod.at[256:384, at], xpeer(1), dst=ferry.at[k]))
+        ferry_on.append(send(ferry.at[k], far, dst=prod.at[0:128, at], slot=slot))
     first = {d: send(strip(y, h, 1, x), ypeer(d)) for d in around}
     second = {(k, d): send(strip(back(y, k), h, 1, x), xpeer(d)) for k in around for d in near}
     second_on = {
@@ -194,7 +197,7 @@
 
     @pl.when(hi)
     def _():
-        hand_on(ferry_out)
+        hand_on(*ferry_out)
 
     @pl.when(jnp.logical_or(zl == 3, jnp.logical_not(passes)))
     def _():
@@ -264,20 +267,22 @@
         hand_on(tails[1])
 
     cross_over(4)
+    for d in near:
+        direct[d].wait_recv()
+        relay[d].start()
+
+    @pl.when(hi)
+    def _():
+        hand_on(heads)
+        for k in (0, 1):
+            ferry_out[k].wait_recv()
+            ferry_on[k].start()
+
     for copy in second.values():
         copy.wait_recv()
     for copy in second_on.values():
         copy.start()
 
-    @pl.when(hi)
-    def _():
-        hand_on(heads, tails[0])
-        ferry_out.wait_recv()
-        ferry_on.start()
-
-    for d in near:
-        direct[d].wait_recv()
-        relay[d].start()
     for d in near:
         mate_direct[d].start()
     for copy in second_on.values():
@@ -290,8 +295,8 @@
         wide0[d].start()
     for d in around:
         spread1[d].wait_recv()
-    wide1[3].start()
-    pl.when(jnp.logical_not(lo))(wide1[1].start)
+    for d in near:
+        wide1[d].start()
     mate_wide0[0].start()
     mate_wide1[0].start()
     for d in near:
@@ -316,12 +321,6 @@
     raw[0:16, :3072] = jnp.concatenate([got[0:8], got[0:8]], axis=0).astype(BF)
     raw[0:16, 3072:] = jnp.concatenate([got[8:16], got[8:16]], axis=0).astype(BF)
 
-    @pl.when(lo)
-    def _():
-        for copy in tails:
-            copy.wait_recv()
-        wide1[1].start()
-
     @pl.loop(0, 16)
     def _(j):
         lane = j * 128
@@ -329,10 +328,8 @@
         query[0:128, cols(lane, 128)] = conv(lane, 0, 2)
         query[128:256, cols(lane, 128)] = conv(lane, 128, 3)
 
-    @pl.when(jnp.logical_not(lo))
-    def _():
-        for copy in tails:
-            copy.wait_recv()
+    for copy in tails:
+        copy.wait_recv()
 
     @pl.when(s == 0)
     def _():
@@ -437,14 +434,15 @@
 
     @pl.when(hi)
     def _():
-        ferry_out.wait_send()
-        ferry_on.wait_send()
+        for copy in (*ferry_out, *ferry_on):
+            copy.wait_send()
 
     @pl.when(jnp.logical_not(hi))
     def _():
-        tails[1].wait_send()
-
-    for copy in (heads, tails[0], mate):
+        for copy in tails:
+            copy.wait_send()
+
+    for copy in (heads, mate):
         copy.wait_send()
     for group_of in (
         first, second, second_on, direct, relay, spread0, spread1, wide0, wide1, relay0, relay1, mate_direct, mate_second, mate_wide0, mate_wide1,
@@ -468,7 +466,7 @@
             pltpu.VMEM((4, 144, 128), F32),
             pltpu.VMEM((2, 16, 3072), BF),
             pltpu.VMEM((384, 2048), BF),
-            pltpu.VMEM((128, 1024), BF),
+            pltpu.VMEM((2, 128, 1024), BF),
             pltpu.VMEM((256, 2048), F32),
             pltpu.VMEM((128, 128), F32),
             pltpu.VMEM((16384, 256), BF),

time: 70.8 us -> 63.9 us (0.903); the launches traced: 70.6 us -> 62.9 us
  Pallas kernels: 69.4 us -> 61.6 us
    pallas_call x1, Pallas kernels: 69.4 us -> 61.6 us  [body(): pl.pallas_call(kernel, name='hyena_block', out_shape=jax.ShapeDtypeStruct...]
where the time goes in v4:
time: 63.9 us; the launch traced here: 62.9 us
  Pallas kernels  61.6 us (96%)
  local copies, waits for them, and re-layouts  1.24 us (2%)
    pallas_call x1, Pallas kernels, body(): pl.pallas_call(kernel, name='hyena_block', out_shape=jax.ShapeDtypeStruct...  61.6 us

profile of v4, /device:TPU:1, one launch (start us, length us, event | category | flops | bytes accessed | tf_op | source)
XLA Modules:
  0.0 62.9 jit_solution(724579574905095788)
XLA Ops:
  0.0 61.6 %hyena_block.1 = f32[1,256]{1,0:T(1,128)} custom-call(bf16[1,256,6144]{2,1,0:T(8,128)(2,1)} %qkv.1, bf16[1,256,2048]{2,1,0:T(8,128)(2,1)} %resid.1, s32[1,256]{1,0:T(1,128)} %targets.1, f32[7,6144]{1,0:T(8,128)} %taps_in.1, bf16[128,128]{1,0:T(8,128)(2,1)} %longs_in.1, f32[1,2048]{1,0:T(1,128)} %bitcast.2, bf16[128,2048]{1,0:T(8,128)(2,1)} %ow.1, ...), custom_call_target="tpu_custom_call" | custom-call | flops 7000000000 | bytes 20000000 | tf_op jit(solution)/shard_map/hyena_block/pallas_call | solution.py:458
  61.6 1.2 %copy.11 = f32[1,256]{1,0:T(1,128)} copy(f32[1,256]{1,0:T(1,128)} %hyena_block.1) | data formatting | bytes 2048

commit v5 on v4

--- a/solution.py
+++ b/solution.py
@@ -22,7 +22,7 @@
 def kernel(
     qkv, resid, targets, taps_in, longs_in, skip_in, ow, gain_in, vw, out,
     raw, ext, pack, prod, ferry, query, flips, mats, gated, wbuf, stream, base, taps, longs, skip, gain, wanted,
-    local_sem, send_sem, recv_sem,
+    local_sem, send_sem, recv_sem, gate_sem,
 ):
     H = 2048
     s, f = lax.axis_index("seq"), lax.axis_index("fsdp")
@@ -70,6 +70,13 @@
     @pl.when(edge)
     def _():
         greet(far)
+
+    guard = zl == 5
+    other = place(x, y, jnp.where(guard, z + 2, z - 2), c)
+
+    @pl.when(jnp.logical_or(guard, hi))
+    def _():
+        greet(other)
 
     loads = []
 
@@ -158,17 +165,6 @@
     mate_relay0 = {d: send(half_whole(back(y, 2), o, d), sibling) for d in near}
     mate_relay1 = {d: send(half_column(back(x, 2), d), sibling) for d in near}
 
-    for copy in load_own:
-        copy.wait()
-    pl.semaphore_wait(barrier, 10 + jnp.where(passes, 1, 0) + jnp.where(edge, 1, 0))
-
-    @pl.when(edge)
-    def _():
-        for copy in cross:
-            copy.start()
-
-    for d in around:
-        first[d].start()
     def conv(col, top, spot):
         ext[spot] = raw[top : top + 144, cols(col, 128)].astype(F32)
         total = jnp.zeros((128, 128), F32)
@@ -181,15 +177,30 @@
         v = conv(2 * H + lane, top, spot + 1)
         prod[128 + top : 256 + top, cols(lane, 128)] = (k * v).astype(BF)
 
-    load_late.wait()
-    load_taps.wait()
-    load_q.wait()
-    last = raw[256:272].astype(F32)[8:16]
-    pack[0] = jnp.concatenate([last[:, :3072], last[:, 3072:]], axis=0).astype(BF)
-
-    @pl.loop(0, 16)
-    def _(j):
-        product(j * 128, 128, 0)
+    def late_rows():
+        load_late.wait()
+        load_taps.wait()
+        load_q.wait()
+        last = raw[256:272].astype(F32)[8:16]
+        pack[0] = jnp.concatenate([last[:, :3072], last[:, 3072:]], axis=0).astype(BF)
+
+        @pl.loop(0, 16)
+        def _(j):
+            product(j * 128, 128, 0)
+
+    pl.when(hi)(late_rows)
+    for copy in load_own:
+        copy.wait()
+    pl.semaphore_wait(barrier, 10 + jnp.where(passes, 1, 0) + jnp.where(edge, 1, 0) + jnp.where(jnp.logical_or(guard, hi), 1, 0))
+
+    @pl.when(edge)
+    def _():
+        for copy in cross:
+            copy.start()
+
+    for d in around:
+        first[d].start()
+    pl.when(jnp.logical_not(hi))(late_rows)
 
     def hand_on(*copies):
         for copy in copies:
@@ -230,8 +241,8 @@
 
     for k in around:
         first[k].wait_recv()
-        for d in near:
-            second[k, d].start()
+        pl.when(jnp.logical_not(hi))(second[k, 1].start)
+        second[k, 3].start()
 
     cross_over(1)
 
@@ -256,6 +267,10 @@
 
     cross_over(2)
 
+    @pl.when(guard)
+    def _():
+        pl.semaphore_signal(gate_sem, inc=1, device_id=other, device_id_type=MESH)
+
     @pl.when(zl == 2)
     def _():
         hand_on(heads, *tails)
@@ -273,10 +288,13 @@
 
     @pl.when(hi)
     def _():
+        pl.semaphore_wait(gate_sem, 1)
         hand_on(heads)
         for k in (0, 1):
             ferry_out[k].wait_recv()
             ferry_on[k].start()
+        for k in around:
+            second[k, 1].start()
 
     for copy in second.values():
         copy.wait_recv()
@@ -328,6 +346,7 @@
         query[0:128, cols(lane, 128)] = conv(lane, 0, 2)
         query[128:256, cols(lane, 128)] = conv(lane, 128, 3)
 
+    pl.when(lo)(pass_wide)
     for copy in tails:
         copy.wait_recv()
 
@@ -362,7 +381,7 @@
         at = tile(half, xx)
         stream[:, at] = stream[:, at] + project(o, half, xx, blocks)
 
-    pass_wide()
+    pl.when(jnp.logical_not(lo))(pass_wide)
     mate.wait_recv()
     for d in around:
         mate_direct[d].wait_recv()
@@ -482,6 +501,7 @@
             pltpu.SemaphoreType.DMA((32,)),
             pltpu.SemaphoreType.DMA((72,)),
             pltpu.SemaphoreType.DMA((72,)),
+            pltpu.SemaphoreType.REGULAR,
         ],
         compiler_params=pltpu.CompilerParams(
             collective_id=0, has_side_effects=True, vmem_limit_bytes=60 << 20

time: 63.9 us -> 63.5 us (level); the launches traced: 62.9 us -> 63.3 us
  no operation moved by 1% of the time
where the time goes in v5:
time: 63.5 us; the launch traced here: 63.3 us
  Pallas kernels  62.1 us (98%)
  local copies, waits for them, and re-layouts  1.24 us (2%)
    pallas_call x1, Pallas kernels, body(): pl.pallas_call(kernel, name='hyena_block', out_shape=jax.ShapeDtypeStruct...  62.1 us

profile of v5, /device:TPU:1, one launch (start us, length us, event | category | flops | bytes accessed | tf_op | source)
XLA Modules:
  0.0 63.3 jit_solution(9126236475578040077)
XLA Ops:
  0.0 62.1 %hyena_block.1 = f32[1,256]{1,0:T(1,128)} custom-call(bf16[1,256,6144]{2,1,0:T(8,128)(2,1)} %qkv.1, bf16[1,256,2048]{2,1,0:T(8,128)(2,1)} %resid.1, s32[1,256]{1,0:T(1,128)} %targets.1, f32[7,6144]{1,0:T(8,128)} %taps_in.1, bf16[128,128]{1,0:T(8,128)(2,1)} %longs_in.1, f32[1,2048]{1,0:T(1,128)} %bitcast.2, bf16[128,2048]{1,0:T(8,128)(2,1)} %ow.1, ...), custom_call_target="tpu_custom_call" | custom-call | flops 7000000000 | bytes 20000000 | tf_op jit(solution)/shard_map/hyena_block/pallas_call | solution.py:477
  62.1 1.2 %copy.11 = f32[1,256]{1,0:T(1,128)} copy(f32[1,256]{1,0:T(1,128)} %hyena_block.1) | data formatting | bytes 2048

commit v6 on v5

--- a/solution.py
+++ b/solution.py
@@ -71,12 +71,7 @@
     def _():
         greet(far)
 
-    guard = zl == 5
-    other = place(x, y, jnp.where(guard, z + 2, z - 2), c)
-
-    @pl.when(jnp.logical_or(guard, hi))
-    def _():
-        greet(other)
+    guard = zl == 6
 
     loads = []
 
@@ -191,7 +186,7 @@
     pl.when(hi)(late_rows)
     for copy in load_own:
         copy.wait()
-    pl.semaphore_wait(barrier, 10 + jnp.where(passes, 1, 0) + jnp.where(edge, 1, 0) + jnp.where(jnp.logical_or(guard, hi), 1, 0))
+    pl.semaphore_wait(barrier, 10 + jnp.where(passes, 1, 0) + jnp.where(edge, 1, 0))
 
     @pl.when(edge)
     def _():
@@ -269,7 +264,9 @@
 
     @pl.when(guard)
     def _():
-        pl.semaphore_signal(gate_sem, inc=1, device_id=other, device_id_type=MESH)
+        for copy in onward:
+            copy.wait_send()
+        pl.semaphore_signal(gate_sem, inc=1, device_id=outer, device_id_type=MESH)
 
     @pl.when(zl == 2)
     def _():
@@ -346,7 +343,18 @@
         query[0:128, cols(lane, 128)] = conv(lane, 0, 2)
         query[128:256, cols(lane, 128)] = conv(lane, 128, 3)
 
-    pl.when(lo)(pass_wide)
+    def pass_relays():
+        for d in near:
+            relay0[d].wait_recv()
+            mate_relay0[d].start()
+            relay1[d].wait_recv()
+            mate_relay1[d].start()
+
+    @pl.when(lo)
+    def _():
+        pass_wide()
+        pass_relays()
+
     for copy in tails:
         copy.wait_recv()
 
@@ -356,7 +364,7 @@
 
     group = lax.broadcasted_iota(jnp.int32, (128, 128), 1) // 16
 
-    @pl.loop(0, 16)
+    @pl.loop(0, 16, unroll=2)
     def _(j):
         lane = cols(j * 128, 128)
         pair = jnp.concatenate([prod[0:256, lane], prod[128:384, lane]], axis=1)
@@ -388,7 +396,7 @@
     for d in around:
         mate_second[d].wait_recv()
 
-    @pl.loop(0, 8)
+    @pl.loop(0, 8, unroll=2)
     def _(n):
         half, xx = n // 4, lax.rem(n, 4)
         at = tile(half, xx)
@@ -398,19 +406,15 @@
         for copy in group_of.values():
             copy.wait_recv()
 
-    @pl.loop(0, 3)
+    @pl.loop(0, 3, unroll=3)
     def _(n):
         gather_in(1, lax.rem(x + 3 + n, 4), range(4))
 
-    @pl.loop(0, 4)
+    @pl.loop(0, 4, unroll=4)
     def _(n):
         gather_in(0, n, [lax.rem(y + 3 + k, 4) for k in range(3)])
 
-    for d in near:
-        relay0[d].wait_recv()
-        mate_relay0[d].start()
-        relay1[d].wait_recv()
-        mate_relay1[d].start()
+    pl.when(jnp.logical_not(lo))(pass_relays)
     for group_of in (mate_relay0, mate_relay1):
         for copy in group_of.values():
             copy.wait_recv()
@@ -424,10 +428,10 @@
             squares = squares + total[:, :128] * total[:, :128] + total[:, 128:] * total[:, 128:]
         return squares
 
-    squares = lax.fori_loop(0, 4, close, jnp.zeros((256, 128), F32))
+    squares = lax.fori_loop(0, 4, close, jnp.zeros((256, 128), F32), unroll=2)
     scale = lax.rsqrt(jnp.sum(squares, axis=1, keepdims=True) / 2048.0 + 1e-05)
 
-    @pl.loop(0, 8)
+    @pl.loop(0, 8, unroll=2)
     def _(n):
         at = cols(n * 256, 256)
         gated[:, at] = (stream[:, at] * scale * gain[:, at]).astype(BF)
@@ -446,7 +450,7 @@
         for copy in cross:
             copy.wait_send()
 
-    @pl.when(passes)
+    @pl.when(jnp.logical_and(passes, jnp.logical_not(guard)))
     def _():
         for copy in onward:
             copy.wait_send()

time: 63.5 us -> 62.4 us (0.983)
  the two profiles are of different devices: /device:TPU:1 before, /device:TPU:8 now
where the time goes in v6:
time: 62.4 us; the launch traced here: 62.2 us
  Pallas kernels  61 us (98%)
  local copies, waits for them, and re-layouts  1.24 us (2%)
    pallas_call x1, Pallas kernels, body(): pl.pallas_call(kernel, name='hyena_block', out_shape=jax.ShapeDtypeStruct...  61 us

profile of v6, /device:TPU:8, one launch (start us, length us, event | category | flops | bytes accessed | tf_op | source)
XLA Modules:
  0.0 62.2 jit_solution(16685108703496710263)
XLA Ops:
  0.0 61.0 %hyena_block.1 = f32[1,256]{1,0:T(1,128)} custom-call(bf16[1,256,6144]{2,1,0:T(8,128)(2,1)} %qkv.1, bf16[1,256,2048]{2,1,0:T(8,128)(2,1)} %resid.1, s32[1,256]{1,0:T(1,128)} %targets.1, f32[7,6144]{1,0:T(8,128)} %taps_in.1, bf16[128,128]{1,0:T(8,128)(2,1)} %longs_in.1, f32[1,2048]{1,0:T(1,128)} %bitcast.2, bf16[128,2048]{1,0:T(8,128)(2,1)} %ow.1, ...), custom_call_target="tpu_custom_call" | custom-call | flops 7000000000 | bytes 20000000 | tf_op jit(solution)/shard_map/hyena_block/pallas_call | solution.py:481
  61.0 1.2 %copy.11 = f32[1,256]{1,0:T(1,128)} copy(f32[1,256]{1,0:T(1,128)} %hyena_block.1) | data formatting | bytes 2048

commit v7 on v6

--- a/solution.py
+++ b/solution.py
@@ -279,17 +279,22 @@
         hand_on(tails[1])
 
     cross_over(4)
+
+    @pl.when(hi)
+    def _():
+        pl.semaphore_wait(gate_sem, 1)
+        hand_on(heads)
+        ferry_out[0].wait_recv()
+        ferry_on[0].start()
+
     for d in near:
         direct[d].wait_recv()
         relay[d].start()
 
     @pl.when(hi)
     def _():
-        pl.semaphore_wait(gate_sem, 1)
-        hand_on(heads)
-        for k in (0, 1):
-            ferry_out[k].wait_recv()
-            ferry_on[k].start()
+        ferry_out[1].wait_recv()
+        ferry_on[1].start()
         for k in around:
             second[k, 1].start()
 

time: 62.4 us -> 62.4 us (level)
  no operation moved by 1% of the time
where the time goes in v7:
time: 62.4 us; the launch traced here: 62.2 us
  Pallas kernels  61 us (98%)
  local copies, waits for them, and re-layouts  1.24 us (2%)
    pallas_call x1, Pallas kernels, body(): pl.pallas_call(kernel, name='hyena_block', out_shape=jax.ShapeDtypeStruct...  61 us

profile of v7, /device:TPU:8, one launch (start us, length us, event | category | flops | bytes accessed | tf_op | source)
XLA Modules:
  0.0 62.2 jit_solution(14365504339840375007)
XLA Ops:
  0.0 61.0 %hyena_block.1 = f32[1,256]{1,0:T(1,128)} custom-call(bf16[1,256,6144]{2,1,0:T(8,128)(2,1)} %qkv.1, bf16[1,256,2048]{2,1,0:T(8,128)(2,1)} %resid.1, s32[1,256]{1,0:T(1,128)} %targets.1, f32[7,6144]{1,0:T(8,128)} %taps_in.1, bf16[128,128]{1,0:T(8,128)(2,1)} %longs_in.1, f32[1,2048]{1,0:T(1,128)} %bitcast.2, bf16[128,2048]{1,0:T(8,128)(2,1)} %ow.1, ...), custom_call_target="tpu_custom_call" | custom-call | flops 7000000000 | bytes 20000000 | tf_op jit(solution)/shard_map/hyena_block/pallas_call | solution.py:486
  61.0 1.2 %copy.11 = f32[1,256]{1,0:T(1,128)} copy(f32[1,256]{1,0:T(1,128)} %hyena_block.1) | data formatting | bytes 2048
